TPU v7x, 256 devices: a whole 4x4x8 slice. The times are simulated.
256 devices in a mesh: dp: 8 (over y, core), ctx: 32 (over z, x).
Axes of the slice: x: 4, y: 4, z: 8, core: 2. Of those that a mesh axis runs over, the one named last changes fastest.
Arguments:
- conv_input: bfloat16 [32768, 7424], P(('dp', 'ctx')), parts along dimension 0, may hold values from -6 to 6
- gate_input: bfloat16 [32768, 7168], P(('dp', 'ctx')), parts along dimension 0, may hold values from -6 to 6
- step_raw: float32 [32768, 112], P(('dp', 'ctx')), parts along dimension 0, may hold values from -2 to 24
- step_bias: float32 [112], replicated, may hold values from -13 to 0
- decay_log: float32 [112], replicated, may hold values from -3.3 to -1.6
- skip_weight: float32 [112], replicated, may hold values from 0.3 to 1.2
- conv_weight: float32 [4, 7424], replicated, may hold values from -3 to 3
- conv_bias: float32 [7424], replicated, may hold values from -3 to 3
- norm_gain: float32 [7168], replicated, may hold values from 0.25 to 1.75
- queries: bfloat16 [32768, 7168], P(('dp', 'ctx')), parts along dimension 0, may hold values from -130 to 130
- key_rows: bfloat16 [32768, 7168], P(('dp', 'ctx')), parts along dimension 0, may hold values from -10 to 10
Outputs:
- mamba_out: bfloat16 [32768, 7168], P(('dp', 'ctx')), parts along dimension 0
- attended: bfloat16 [32768, 7168], P(('dp', 'ctx')), parts along dimension 0
There are 8 independent parts, one for each index of `dp`. A program takes and returns all parts, laid end to end along the dimension named above; an argument that names none is the same for every part. Nothing has to cross between parts.
All inputs are finite; a program needn't handle non-finite values.
Results may differ from a plain program's by a relative error of at most 0.005.
Values may be sent and summed in bfloat16 or wider, within the bound.
No kernel may reach another device: no remote copies, remote signals or barrier semaphores. Data moves between devices by JAX's collectives and lax.ppermute only.
A program may use at most 320 MiB of HBM per device.

v0:
```python
import math

import jax
import jax.numpy as jnp
from jax import lax
from jax.sharding import PartitionSpec as P

HEADS = 112
HEAD_DIM = 64
STATE = 64
GROUPS = 2
CONV = 4
ATT_DIM = 224


dt_cap = 3.0
eps = 1e-05


def shifted(array, axis, by):
    size = lax.axis_size(axis)
    pairs = [(i, i + by) for i in range(size) if 0 <= i + by < size]
    return lax.ppermute(array, axis, pairs)


def carried_in(array, axis, combine, identity):
    size, index = (lax.axis_size(axis), lax.axis_index(axis))
    everything = jax.tree.map(lambda part: lax.all_gather(part, axis), array)
    start = jax.tree.map(
        lambda part, zero: jnp.broadcast_to(jnp.asarray(zero, part.dtype), part.shape),
        array,
        identity,
    )

    def step(k, before):
        reached = k < index
        new = combine(before, jax.tree.map(lambda part: part[k], everything))
        return jax.tree.map(lambda a, b: jnp.where(reached, a, b), new, before)

    return lax.fori_loop(0, size, step, start)


def convolve(padded, conv_weight, conv_bias, row_count):
    total = conv_bias[None, :] + conv_weight[0][None, :] * padded[0:row_count]
    for tap_index in range(1, conv_weight.shape[0]):
        total = total + conv_weight[tap_index][None, :] * padded[tap_index : tap_index + row_count]
    return jax.nn.silu(total).astype(jnp.bfloat16)


def span_terms(inputs, step_rates, decay_rate):
    row_count = inputs.shape[0]
    inner_width = HEADS * HEAD_DIM
    head_share = HEADS // GROUPS
    values = (
        inputs[:, :inner_width].astype(jnp.float32).reshape(row_count, GROUPS, head_share, HEAD_DIM)
    )
    writes_low = inputs[:, inner_width : inner_width + GROUPS * STATE].reshape(
        row_count, GROUPS, STATE
    )
    readout_low = inputs[:, inner_width + GROUPS * STATE :].reshape(row_count, GROUPS, STATE)
    writes = writes_low.astype(jnp.float32)
    readout = readout_low.astype(jnp.float32)
    grouped_rates = step_rates.reshape(row_count, GROUPS, head_share)
    running = jnp.cumsum(grouped_rates * decay_rate.reshape(GROUPS, head_share)[None], axis=0)
    running_heads = running.transpose(1, 2, 0)
    rates_heads = grouped_rates.transpose(1, 2, 0)
    positions = jnp.arange(row_count, dtype=jnp.int32)
    causal = (positions[:, None] >= positions[None, :])[None, None]
    spread = running_heads[:, :, :, None] - running_heads[:, :, None, :]
    fading = jnp.exp(jnp.where(causal, spread, -jnp.inf))
    intersection = jnp.einsum(
        "tgn,sgn->gts", readout_low, writes_low, preferred_element_type=jnp.float32
    )
    mixing = intersection[:, None] * fading * rates_heads[:, :, None, :]
    inside = jnp.einsum("gkts,sgkp->tgkp", mixing, values, precision=lax.Precision.HIGHEST)
    trailing_decay = jnp.exp(running[-1])
    carry_weight = jnp.exp(running[-1][None] - running) * grouped_rates
    local_state = jnp.einsum(
        "sgk,sgkp,sgn->gkpn", carry_weight, values, writes, precision=lax.Precision.HIGHEST
    )
    return (values, readout, running, inside, trailing_decay, local_state)


def carried(readout, running, state_in):
    across = jnp.einsum("tgn,gkpn->tgkp", readout, state_in, precision=lax.Precision.HIGHEST)
    return across * jnp.exp(running)[..., None]


def gated_norm(state_output, gate_input, norm_gain):
    row_count = state_output.shape[0]
    gate_values = gate_input.astype(jnp.float32).reshape(row_count, GROUPS, -1)
    gated_values = state_output.reshape(row_count, GROUPS, -1) * jax.nn.silu(gate_values)
    norm_scale = lax.rsqrt(jnp.mean(gated_values * gated_values, axis=-1, keepdims=True) + eps)
    normed = gated_values * norm_scale * norm_gain.reshape(GROUPS, -1)[None]
    return normed.reshape(row_count, -1).astype(jnp.bfloat16)


def link_states(earlier, later):
    return (earlier[0] * later[0], later[0][:, :, None, None] * earlier[1] + later[1])


def attend(head_queries, head_keys, head_values):
    total_rows = head_queries.shape[0]
    local_heads = head_queries.shape[1] // ATT_DIM
    query_all = head_queries.reshape(total_rows, local_heads, ATT_DIM)
    key_all = head_keys.reshape(total_rows, local_heads, ATT_DIM)
    value_all = head_values.reshape(total_rows, local_heads, ATT_DIM)
    score_scale = 1.0 / math.sqrt(ATT_DIM)
    block_rows = total_rows // 8
    pieces = []
    for block_index in range(8):
        block_stop = (block_index + 1) * block_rows
        query_block = query_all[block_index * block_rows : block_stop]
        scores = (
            jnp.einsum(
                "qhd,khd->hqk",
                query_block,
                key_all[:block_stop],
                preferred_element_type=jnp.float32,
            )
            * score_scale
        )
        query_pos = block_index * block_rows + jnp.arange(block_rows, dtype=jnp.int32)
        key_pos = jnp.arange(block_stop, dtype=jnp.int32)
        scores = jnp.where(key_pos[None, None, :] <= query_pos[None, :, None], scores, -jnp.inf)
        row_max = jnp.max(scores, axis=2, keepdims=True)
        exponent = jnp.exp(scores - row_max)
        weights = (exponent / jnp.sum(exponent, axis=2, keepdims=True)).astype(jnp.bfloat16)
        result = jnp.einsum(
            "hqk,khd->qhd", weights, value_all[:block_stop], preferred_element_type=jnp.float32
        )
        pieces.append(result.astype(jnp.bfloat16).reshape(block_rows, local_heads * ATT_DIM))
    return jnp.concatenate(pieces, axis=0)


def local(
    conv_input,
    gate_input,
    step_raw,
    step_bias,
    decay_log,
    skip_weight,
    conv_weight,
    conv_bias,
    norm_gain,
    queries,
    key_rows,
):
    row_count = conv_input.shape[0]
    before = shifted(conv_input[row_count - (CONV - 1) :], "ctx", 1)
    padded = jnp.concatenate([before.astype(jnp.float32), conv_input.astype(jnp.float32)], axis=0)
    inputs = convolve(padded, conv_weight, conv_bias, row_count)
    step_rates = jnp.minimum(jax.nn.softplus(step_raw + step_bias[None, :]), dt_cap)
    decay_rate = -jnp.exp(decay_log)
    skip_gain = skip_weight.reshape(GROUPS, HEADS // GROUPS)[None, :, :, None]
    values, readout, running, inside, trailing_decay, local_state = span_terms(
        inputs, step_rates, decay_rate
    )
    unit_decay = jnp.ones_like(trailing_decay)
    zero_state = jnp.zeros_like(local_state)
    decay_before, state_in = carried_in(
        (trailing_decay, local_state), "ctx", link_states, (unit_decay, zero_state)
    )
    state_output = inside + carried(readout, running, state_in) + skip_gain * values
    mamba_out = gated_norm(state_output, gate_input, norm_gain)
    head_queries, head_keys, head_values = (
        lax.all_to_all(queries, "ctx", split_axis=1, concat_axis=0, tiled=True),
        lax.all_to_all(key_rows, "ctx", split_axis=1, concat_axis=0, tiled=True),
        lax.all_to_all(mamba_out, "ctx", split_axis=1, concat_axis=0, tiled=True),
    )
    attended_heads = attend(head_queries, head_keys, head_values)
    attended = lax.all_to_all(attended_heads, "ctx", split_axis=0, concat_axis=1, tiled=True)
    return (mamba_out, attended)


def solution(mesh):
    placed = (
        P(("dp", "ctx"), None),
        P(("dp", "ctx"), None),
        P(("dp", "ctx"), None),
        P(),
        P(),
        P(),
        P(),
        P(),
        P(),
        P(("dp", "ctx"), None),
        P(("dp", "ctx"), None),
    )
    return jax.shard_map(
        local,
        mesh=mesh,
        in_specs=placed,
        out_specs=(P(("dp", "ctx"), None), P(("dp", "ctx"), None)),
        check_vma=False,
    )
```

profile of v0, /device:TPU:16, one launch (start us, length us, event | category | flops | bytes accessed | tf_op | source)
XLA Modules:
  0.0 1186.4 jit_solution(4970532870404981121)
XLA Ops:
  8.1 3.4 collective-permute-start
  15.2 3.6 convert_element_type.123
  19.0 7.4 multiply_convert_fusion
  26.6 2.3 copy.64
  29.0 5.4 fusion.22
  34.4 2.3 copy.77
  36.7 11.0 all-to-all-start.2
  47.8 4.0 copy.75
  51.8 57.8 %all-to-all-done.2 = bf16[128,32,224]{0,2,1:T(8,128)(2,1)S(1)} async-done(((bf16[128,32,224]{0,2,1:T(8,128)(2,1)}), bf16[128,32,224]{0,2,1:T(8,128)(2,1)S(1)}, u32[]{:S(2)}, u32[]{:S(2)}) %all-to-all-start.2) | async-done | bytes 1835040 | tf_op jit(solution)/shard_map/all_to_all | solution.py:168
  110.8 5.2 all-to-all-start.1
  117.5 3.9 copy.73
  121.4 92.9 %all_gather.10 = f32[32,2,56]{2,1,0:T(2,128)} all-gather(f32[1,2,56]{2,1,0:T(2,128)S(1)} %get-tuple-element.146), channel_id=1, replica_groups=mesh['dp'=8,'ctx'=32] {'ctx'}, dimensions={0}, use_global_device_ids=true | all-gather | bytes 14784 | tf_op jit(solution)/shard_map/all_gather | solution.py:28
  216.4 10.6 fusion.2
  238.6 597.8 %all-gather.3.cloned.1.call-done = f32[64,56,64,64]{3,2,1,0:T(8,128)} async-done(((f32[2,56,64,64]{3,2,1,0:T(8,128)}), f32[64,56,64,64]{3,2,1,0:T(8,128)}) %all-gather.3.cloned.1.call-update) | async-done | bytes 58720272 | tf_op jit(solution)/shard_map/all_gather | solution.py:28
  836.4 199.1 %while.14 = (s32[]{:T(128)}, f32[2,56,64,64]{3,2,1,0:T(8,128)}, s32[]{:T(128)}, f32[32,2,56]{2,1,0:T(2,128)}, f32[32,2,56,64,64]{4,3,2,1,0:T(8,128)}, /*index=5*/s32[]{:T(128)}, s32[]{:T(128)}) while((s32[]{:T(128)}, f32[2,56,64,64]{3,2,1,0:T(8,128)}, s32[]{:T(128)}, f32[32,2,56]{2,1,0:T(2,128)}, f32[32,2,56,64,64]{4,3,2,1,0:T(8,128)}, ...), condition=%wide.region_2.3_spmd.clone, body=%wide.region_1.2_spmd.clone.sunk | while | flops 1835012 | bytes 5506481 | solution.py:40
  837.2 4.5 fusion.158
  842.3 5.6 fusion.158
  848.5 5.6 fusion.158
  854.7 5.6 fusion.158
  861.0 5.6 fusion.158
  867.2 5.6 fusion.158
  873.4 5.6 fusion.158
  879.6 5.6 fusion.158
  885.9 5.6 fusion.158
  892.1 5.6 fusion.158
  898.4 5.6 fusion.158
  904.7 5.6 fusion.158
  910.9 5.6 fusion.158
  917.1 5.6 fusion.158
  923.4 5.6 fusion.158
  929.6 5.6 fusion.158
  935.9 5.6 fusion.158
  942.1 5.6 fusion.158
  948.4 5.6 fusion.158
  954.6 5.6 fusion.158
  960.9 5.6 fusion.158
  967.1 5.6 fusion.158
  973.4 5.6 fusion.158
  979.6 5.6 fusion.158
  985.8 5.6 fusion.158
  992.0 5.6 fusion.158
  998.3 5.6 fusion.158
  1004.5 5.6 fusion.158
  1010.7 5.6 fusion.158
  1016.9 5.6 fusion.158
  1023.2 5.6 fusion.158
  1029.4 5.6 fusion.158
  1035.6 7.3 multiply_reduce_fusion
  1042.9 2.7 fusion.25
  1045.6 6.0 all-to-all-start
  1065.8 3.2 copy-done
  1070.3 25.4 %all-to-all-done = bf16[128,32,224]{0,2,1:T(8,128)(2,1)} async-done(((bf16[128,32,224]{0,2,1:T(8,128)(2,1)}), bf16[128,32,224]{0,2,1:T(8,128)(2,1)}, u32[]{:S(2)}, u32[]{:S(2)}) %all-to-all-start) | async-done | bytes 1835040 | tf_op jit(solution)/shard_map/all_to_all | solution.py:169
  1097.0 2.4 fusion.68
  1100.6 2.5 fusion.86
  1105.4 3.4 fusion.70
  1108.9 3.4 fusion.84
  1112.3 3.7 fusion.92
  1116.1 4.0 fusion.80
  1120.1 4.1 fusion.74
  1124.2 3.1 copy_bitcast_fusion
  1127.3 5.9 all-to-all-start.3
  1133.2 3.9 copy.101
  1137.0 39.4 %all-to-all-done.3 = bf16[32,128,224]{1,2,0:T(8,128)(2,1)S(1)} async-done(((bf16[32,128,224]{1,2,0:T(8,128)(2,1)}), bf16[32,128,224]{1,2,0:T(8,128)(2,1)S(1)}, u32[]{:S(2)}, u32[]{:S(2)}) %all-to-all-start.3) | async-done | bytes 1835040 | tf_op jit(solution)/shard_map/all_to_all | solution.py:172
  1176.5 2.9 copy.102
  (175 shorter events, 62.8 us)
Async XLA Ops:
  7.2 829.2 %all-gather.3.cloned.1.call-start = ((), (), s32[]{:S(2)}) async-start(), calls=%async_computation.4 | async-start | bytes 121110528 | tf_op jit(solution)/shard_map/all_gather | solution.py:28
  8.1 10.8 collective-permute-start
  13.4 5.5 copy-start.23
  29.0 5.4 copy-start.14
  36.7 72.8 %all-to-all-start.2 = ((bf16[128,32,224]{0,2,1:T(8,128)(2,1)}), bf16[128,32,224]{0,2,1:T(8,128)(2,1)S(1)}, u32[]{:S(2)}, u32[]{:S(2)}) async-start(bf16[128,32,224]{0,2,1:T(8,128)(2,1)} %bitcast.21), calls=%async_computation.2 | async-start | bytes 3670016 | tf_op jit(solution)/shard_map/all_to_all | solution.py:168
  47.8 68.3 %copy-start.31 = (f32[112]{0:T(128)S(1)}, f32[112]{0:T(128)}, u32[]{:S(2)}) copy-start(f32[112]{0:T(128)} %param.18) | copy-start | bytes 1348
  109.5 1.3 copy-start.7
  110.8 117.6 %all-to-all-start.1 = ((bf16[128,32,224]{0,2,1:T(8,128)(2,1)}), bf16[128,32,224]{0,2,1:T(8,128)(2,1)S(1)}, u32[]{:S(2)}, u32[]{:S(2)}) async-start(bf16[128,32,224]{0,2,1:T(8,128)(2,1)} %bitcast.331), calls=%async_computation.1 | async-start | bytes 3670016 | tf_op jit(solution)/shard_map/all_to_all | solution.py:167
  216.1 10.8 copy-start.20
  228.4 1.8 copy-start.8
  229.3 2.8 copy-start.27
  230.8 1.3 copy-start.12
  230.8 3.0 copy-start.28
  233.2 1.6 copy-start.10
  233.2 1.6 copy-start.26
  234.8 816.8 %copy-start.15 = (f32[512,512]{0,1:T(8,128)}, f32[512,512]{0,1:T(8,128)S(1)}, u32[]{:S(2)}) copy-start(f32[512,512]{0,1:T(8,128)S(1)} %get-tuple-element.150) | copy-start | bytes 3145732
  235.9 2.0 copy-start.5
  836.4 199.1 %copy-start.2 = (bf16[128,7168]{0,1:T(8,128)(2,1)S(1)}, bf16[128,7168]{0,1:T(8,128)(2,1)}, u32[]{:S(2)}) copy-start(bf16[128,7168]{0,1:T(8,128)(2,1)} %copy.73) | copy-start | bytes 5505028
  836.4 199.1 %copy-start.21 = (bf16[128,128]{0,1:T(8,128)(2,1)S(1)}, bf16[128,128]{0,1:T(8,128)(2,1)}, u32[]{:S(2)}) copy-start(bf16[128,128]{0,1:T(8,128)(2,1)} %copy-done.20) | copy-start | bytes 98308
  836.4 199.2 %copy-start.22 = (f32[128,2,56]{0,2,1:T(8,128)S(1)}, f32[128,2,56]{0,2,1:T(8,128)}, u32[]{:S(2)}) copy-start(f32[128,2,56]{0,2,1:T(8,128)} %copy.72) | copy-start | bytes 172036
  836.4 199.2 %copy-start.32 = (f32[2,56]{1,0:T(2,128)S(1)}, f32[2,56]{1,0:T(2,128)}, u32[]{:S(2)}) copy-start(f32[2,56]{1,0:T(2,128)} %mul.233) | copy-start | bytes 1348
  1035.5 7.4 copy-start.24
  1045.6 6.3 copy-start.9
  1045.6 6.3 copy-start.19
  1045.6 6.3 copy-start.25
  1045.6 50.1 %all-to-all-start = ((bf16[128,32,224]{0,2,1:T(8,128)(2,1)}), bf16[128,32,224]{0,2,1:T(8,128)(2,1)}, u32[]{:S(2)}, u32[]{:S(2)}) async-start(bf16[128,32,224]{0,2,1:T(8,128)(2,1)} %bitcast.17), calls=%async_computation | async-start | bytes 3670016 | tf_op jit(solution)/shard_map/all_to_all | solution.py:169
  1053.0 2.3 copy-start.4
  1053.1 2.3 copy-start.18
  1056.8 2.6 copy-start.3
  1056.8 2.6 copy-start.17
  1061.0 3.0 copy-start.1
  1065.8 3.2 copy-start
  1095.7 4.9 copy-start.13
  1095.7 4.9 copy-start.29
  1095.7 4.9 copy-start.30
  1100.6 2.5 copy-start.11
  1100.6 2.5 copy-start.16
  1103.1 2.3 copy-start.6
  1103.1 5.7 slice-start.6
  1105.4 3.5 slice-start.7
  1105.4 6.9 slice-start.4
  1108.9 3.4 slice-start.5
  1108.9 7.2 slice-start.2
  1112.3 3.7 slice-start.3
  1112.3 7.7 slice-start
  1116.1 4.0 slice-start.1
  1127.3 49.2 %all-to-all-start.3 = ((bf16[32,128,224]{1,2,0:T(8,128)(2,1)}), bf16[32,128,224]{1,2,0:T(8,128)(2,1)S(1)}, u32[]{:S(2)}, u32[]{:S(2)}) async-start(bf16[32,128,224]{1,2,0:T(8,128)(2,1)} %copy_bitcast_fusion), calls=%async_computation.3 | async-start | bytes 3670016 | tf_op jit(solution)/shard_map/all_to_all | solution.py:172
Sparse Core Ops, SparseCore 0:
  34.5 801.7 all-gather.2
where the time goes:
time: 1190 us
  waiting for transfers between devices  720 us (61%)
  other arithmetic  202 us (17%)
  blocking collectives  92.9 us (8%)
  local copies, waits for them, and re-layouts  66.6 us (6%)
  matrix products  57.9 us (5%)
  starting transfers between devices  31.6 us (3%)
  between operations  14.7 us (1%)
    all_gather x1, waiting for transfers between devices, carried_in(): everything = jax.tree.map(lambda part: lax.all_gather(part, axis), array)  598 us
    select_n x32, other arithmetic, step(): return jax.tree.map(lambda a, b: jnp.where(reached, a, b), new, before)  177 us
    all_gather x1, blocking collectives, carried_in(): everything = jax.tree.map(lambda part: lax.all_gather(part, axis), array)  92.9 us
    all_to_all x1, waiting for transfers between devices, local(): lax.all_to_all(key_rows, 'ctx', split_axis=1, concat_axis=0, tiled=True)  57.8 us
    all_to_all x1, waiting for transfers between devices, local(): lax.all_to_all(attended_heads, 'ctx', split_axis=0, concat_axis=1, tiled=...  39.4 us
    unnamed x89, local copies, waits for them, and re-layouts  31.6 us
    all_to_all x1, waiting for transfers between devices, local(): lax.all_to_all(mamba_out, 'ctx', split_axis=1, concat_axis=0, tiled=True)  25.4 us
    dot_general x8, matrix products, attend(): jnp.einsum('hqk,khd->qhd', weights, value_all[:block_stop], preferred_ele...  25.3 us
  transfers between devices with their start and end apart: 6, of which 4 were waited for; matrix products, arithmetic and copies ran while one was open for 5% of the time, Pallas kernels for 0%

commit v1 on v0

v1 whole, which is shorter than its diff:
```python
import math

import jax
import jax.numpy as jnp
from jax import lax
from jax.experimental import pallas as pl
from jax.experimental.pallas import tpu as pltpu
from jax.sharding import PartitionSpec as P

HEADS = 112
HEAD_DIM = 64
STATE = 64
GROUPS = 2
CONV = 4
ATT_DIM = 224
INNER = HEADS * HEAD_DIM
ROW_PARTS = 4
COL_PARTS = 8
PART_ROWS = STATE // ROW_PARTS
PART_COLS = INNER // COL_PARTS

dt_cap = 3.0
eps = 1e-05
HIGHEST = lax.Precision.HIGHEST


def shifted(array, axis, by):
    size = lax.axis_size(axis)
    pairs = [(i, i + by) for i in range(size) if 0 <= i + by < size]
    return lax.ppermute(array, axis, pairs)


def convolve(padded, conv_weight, conv_bias, row_count):
    total = conv_bias[None, :] + conv_weight[0][None, :] * padded[0:row_count]
    for tap_index in range(1, conv_weight.shape[0]):
        total = total + conv_weight[tap_index][None, :] * padded[tap_index : tap_index + row_count]
    return jax.nn.silu(total).astype(jnp.bfloat16)


def scan_kernel(decay_ref, state_ref, out_ref):
    state = jnp.zeros(state_ref.shape[1:], jnp.float32)
    for block in range(state_ref.shape[0]):
        out_ref[block] = state.astype(out_ref.dtype)
        state = state * decay_ref[block] + state_ref[block].astype(jnp.float32)


def states_before(local_state, block_decay):
    size, index = lax.axis_size("ctx"), lax.axis_index("ctx")
    parts = local_state.astype(jnp.bfloat16).reshape(ROW_PARTS, PART_ROWS, COL_PARTS, PART_COLS)
    parts = parts.transpose(0, 2, 1, 3).reshape(size, PART_ROWS, PART_COLS)
    all_decay = lax.all_gather(block_decay, "ctx")
    heads = PART_COLS // HEAD_DIM
    own_decay = lax.dynamic_slice_in_dim(all_decay, (index % COL_PARTS) * heads, heads, 1)
    own_decay = jnp.repeat(own_decay, HEAD_DIM, axis=1)[:, None, :]
    blocks = lax.all_to_all(parts, "ctx", 0, 0, tiled=True)
    before = pl.pallas_call(
        scan_kernel,
        out_shape=jax.ShapeDtypeStruct(blocks.shape, jnp.bfloat16),
        compiler_params=pltpu.CompilerParams(vmem_limit_bytes=32 * 1024 * 1024),
    )(own_decay, blocks)
    state_in = lax.all_to_all(before, "ctx", 0, 0, tiled=True)
    state_in = state_in.reshape(ROW_PARTS, COL_PARTS, PART_ROWS, PART_COLS).transpose(0, 2, 1, 3)
    return state_in.reshape(STATE, INNER)


def gated_norm(state_output, gate_input, norm_gain):
    row_count = state_output.shape[0]
    gate_values = gate_input.astype(jnp.float32).reshape(row_count, GROUPS, -1)
    gated_values = state_output.reshape(row_count, GROUPS, -1) * jax.nn.silu(gate_values)
    norm_scale = lax.rsqrt(jnp.mean(gated_values * gated_values, axis=-1, keepdims=True) + eps)
    normed = gated_values * norm_scale * norm_gain.reshape(GROUPS, -1)[None]
    return normed.reshape(row_count, -1).astype(jnp.bfloat16)


def attend(head_queries, head_keys, head_values):
    total_rows = head_queries.shape[0]
    local_heads = head_queries.shape[1] // ATT_DIM
    query_all = head_queries.reshape(total_rows, local_heads, ATT_DIM)
    key_all = head_keys.reshape(total_rows, local_heads, ATT_DIM)
    value_all = head_values.reshape(total_rows, local_heads, ATT_DIM)
    score_scale = 1.0 / math.sqrt(ATT_DIM)
    block_rows = total_rows // 8
    pieces = []
    for block_index in range(8):
        block_stop = (block_index + 1) * block_rows
        query_block = query_all[block_index * block_rows : block_stop]
        scores = (
            jnp.einsum(
                "qhd,khd->hqk",
                query_block,
                key_all[:block_stop],
                preferred_element_type=jnp.float32,
            )
            * score_scale
        )
        query_pos = block_index * block_rows + jnp.arange(block_rows, dtype=jnp.int32)
        key_pos = jnp.arange(block_stop, dtype=jnp.int32)
        scores = jnp.where(key_pos[None, None, :] <= query_pos[None, :, None], scores, -jnp.inf)
        row_max = jnp.max(scores, axis=2, keepdims=True)
        exponent = jnp.exp(scores - row_max)
        weights = (exponent / jnp.sum(exponent, axis=2, keepdims=True)).astype(jnp.bfloat16)
        result = jnp.einsum(
            "hqk,khd->qhd", weights, value_all[:block_stop], preferred_element_type=jnp.float32
        )
        pieces.append(result.astype(jnp.bfloat16).reshape(block_rows, local_heads * ATT_DIM))
    return jnp.concatenate(pieces, axis=0)


def local(
    conv_input,
    gate_input,
    step_raw,
    step_bias,
    decay_log,
    skip_weight,
    conv_weight,
    conv_bias,
    norm_gain,
    queries,
    key_rows,
):
    row_count = conv_input.shape[0]
    share = HEADS // GROUPS
    before = shifted(conv_input[row_count - (CONV - 1) :], "ctx", 1)
    padded = jnp.concatenate([before.astype(jnp.float32), conv_input.astype(jnp.float32)], axis=0)
    inputs = convolve(padded, conv_weight, conv_bias, row_count)
    step_rates = jnp.minimum(jax.nn.softplus(step_raw + step_bias[None, :]), dt_cap)
    decay_rate = -jnp.exp(decay_log)
    running = jnp.cumsum(step_rates * decay_rate[None], axis=0)
    values = inputs[:, :INNER].astype(jnp.float32)
    writes = inputs[:, INNER : INNER + GROUPS * STATE].reshape(row_count, GROUPS, STATE)
    readout = inputs[:, INNER + GROUPS * STATE :].reshape(row_count, GROUPS, STATE)
    carry_weight = jnp.exp(running[-1][None] - running) * step_rates
    weighted = values * jnp.repeat(carry_weight, HEAD_DIM, axis=1)
    local_state = jnp.concatenate(
        [
            jnp.einsum(
                "sn,sc->nc",
                writes[:, g].astype(jnp.float32),
                weighted[:, g * share * HEAD_DIM : (g + 1) * share * HEAD_DIM],
                precision=HIGHEST,
            )
            for g in range(GROUPS)
        ],
        axis=1,
    )
    state_in = states_before(local_state, jnp.exp(running[-1]))

    running_heads = running.T.reshape(GROUPS, share, row_count)
    rates_heads = step_rates.T.reshape(GROUPS, share, row_count)
    positions = jnp.arange(row_count, dtype=jnp.int32)
    causal = (positions[:, None] >= positions[None, :])[None, None]
    spread = running_heads[:, :, :, None] - running_heads[:, :, None, :]
    fading = jnp.exp(jnp.where(causal, spread, -jnp.inf))
    intersection = jnp.einsum("tgn,sgn->gts", readout, writes, preferred_element_type=jnp.float32)
    mixing = intersection[:, None] * fading * rates_heads[:, :, None, :]
    grouped = values.reshape(row_count, GROUPS, share, HEAD_DIM)
    inside = jnp.einsum("gkts,sgkp->tgkp", mixing, grouped, precision=HIGHEST)
    state_output = inside.reshape(row_count, INNER) + jnp.repeat(skip_weight, HEAD_DIM)[None] * values

    across = jnp.concatenate(
        [
            jnp.einsum(
                "tn,nc->tc",
                readout[:, g],
                state_in[:, g * share * HEAD_DIM : (g + 1) * share * HEAD_DIM],
                preferred_element_type=jnp.float32,
            )
            for g in range(GROUPS)
        ],
        axis=1,
    )
    state_output = state_output + across * jnp.repeat(jnp.exp(running), HEAD_DIM, axis=1)
    mamba_out = gated_norm(state_output, gate_input, norm_gain)
    head_queries, head_keys, head_values = (
        lax.all_to_all(queries, "ctx", split_axis=1, concat_axis=0, tiled=True),
        lax.all_to_all(key_rows, "ctx", split_axis=1, concat_axis=0, tiled=True),
        lax.all_to_all(mamba_out, "ctx", split_axis=1, concat_axis=0, tiled=True),
    )
    attended_heads = attend(head_queries, head_keys, head_values)
    attended = lax.all_to_all(attended_heads, "ctx", split_axis=0, concat_axis=1, tiled=True)
    return (mamba_out, attended)


def solution(mesh):
    rows = P(("dp", "ctx"), None)
    placed = (rows, rows, rows, P(), P(), P(), P(), P(), P(), rows, rows)
    return jax.shard_map(
        local, mesh=mesh, in_specs=placed, out_specs=(rows, rows), check_vma=False
    )
```

time: 1190 us -> 417 us (0.35)
  waiting for transfers between devices: 720 us -> 71.1 us
  other arithmetic: 202 us -> 35.8 us
  blocking collectives: 92.9 us -> 111 us
  local copies, waits for them, and re-layouts: 66.6 us -> 82.6 us
  between operations: 14.7 us -> 1.39 us
    all_gather x1 -> x0, waiting for transfers between devices: 598 us -> none  [carried_in(): everything = jax.tree.map(lambda part: lax.all_gather(part, axis), array)]
    select_n x32 -> x0, other arithmetic: 177 us -> none  [step(): return jax.tree.map(lambda a, b: jnp.where(reached, a, b), new, before)]
    all_to_all x1, waiting for transfers between devices: 57.8 us -> 0.01 us  [local(): lax.all_to_all(key_rows, 'ctx', split_axis=1, concat_axis=0, tiled=True)]
    all_to_all x0 -> x1, blocking collectives: none -> 40.5 us  [local(): lax.all_to_all(attended_heads, 'ctx', split_axis=0, concat_axis=1, tiled=...]
    all_to_all x1, waiting for transfers between devices: 0.01 us -> 39.5 us  [local(): lax.all_to_all(queries, 'ctx', split_axis=1, concat_axis=0, tiled=True)]
    reshape x1 -> x6, local copies, waits for them, and re-layouts: 0.11 us -> 27.9 us  [the longest x1 6.06 us: gated_norm(): state_output.reshape(row_count, GROUPS, -1) * jax.nn.silu(gate_values)]
    all_gather x1, blocking collectives: 92.9 us -> 70.8 us  [states_before(): all_decay = lax.all_gather(block_decay, 'ctx')]
    mul x36 -> x3, local copies, waits for them, and re-layouts: 22.1 us -> 1.77 us  [the longest x1 1.01 us: gated_norm(): normed = gated_values * norm_scale * norm_gain.reshape(GROUPS, -1)[None]]
  transfers between devices with their start and end apart: 6 -> 6, of which waited for: 4 -> 3; matrix products, arithmetic and copies ran while one was open for 5% -> 23% of each run, Pallas kernels for 0% -> 0%
where the time goes in v1:
time: 417 us; the launch traced here: 409 us
  blocking collectives  111 us (27%)
  local copies, waits for them, and re-layouts  82.6 us (20%)
  waiting for transfers between devices  71.1 us (17%)
  matrix products  63.7 us (15%)
  starting transfers between devices  42.7 us (10%)
  other arithmetic  35.8 us (9%)
    all_gather x1, blocking collectives, states_before(): all_decay = lax.all_gather(block_decay, 'ctx')  70.8 us
    all_to_all x1, blocking collectives, local(): lax.all_to_all(attended_heads, 'ctx', split_axis=0, concat_axis=1, tiled=...  40.5 us
    all_to_all x1, waiting for transfers between devices, local(): lax.all_to_all(queries, 'ctx', split_axis=1, concat_axis=0, tiled=True)  39.5 us
    unnamed x78, local copies, waits for them, and re-layouts  31.2 us
    dot_general x8, matrix products, attend(): jnp.einsum('hqk,khd->qhd', weights, value_all[:block_stop], preferred_ele...  25.6 us
    dot_general x8, matrix products, attend(): jnp.einsum('qhd,khd->hqk', query_block, key_all[:block_stop], preferred_e...  21.9 us
    all_to_all x1, waiting for transfers between devices, states_before(): blocks = lax.all_to_all(parts, 'ctx', 0, 0, tiled=True)  21.3 us
    all_to_all x1, starting transfers between devices, states_before(): blocks = lax.all_to_all(parts, 'ctx', 0, 0, tiled=True)  11 us
  transfers between devices with their start and end apart: 6, of which 3 were waited for; matrix products, arithmetic and copies ran while one was open for 23% of the time, Pallas kernels for 0%

profile of v1, /device:TPU:16, one launch (start us, length us, event | category | flops | bytes accessed | tf_op | source)
XLA Modules:
  0.0 409.5 jit_solution(13280347656337555505)
XLA Ops:
  1.6 3.4 collective-permute-start
  8.2 1.5 slice_reduce_fusion.3
  9.6 3.6 convert_element_type.130
  13.3 2.2 broadcast_in_dim.54
  15.5 5.3 %copy.159 = f32[128,7168]{1,0:T(8,128)} copy(f32[128,7168]{0,1:T(8,128)} %bitcast.314) | data formatting | bytes 7340032 | tf_op jit(solution)/shard_map/reshape | solution.py:134
  20.8 7.6 %multiply_convert_fusion = bf16[128,7424]{1,0:T(8,128)(2,1)S(1)} fusion(f32[128,7424]{1,0:T(8,128)} %convert_element_type.130, f32[3,7424]{1,0:T(4,128)S(1)} %convert_element_type.129, f32[7424]{0:T(1024)S(1)} %get-tuple-element.12, f32[7424]{0:T(1024)S(1)} %get-tuple-element.13, f32[7424]{0:T(1024)S(1)} %get-tuple-element.11, ...), kind=kLoop, calls=%fused_computation.49 | loop fusion | flops 15204352 | bytes 5939200 | tf_op jit(solution)/shard_map/convert_element_type | solution.py:37
  28.4 2.3 convert_multiply_fusion
  30.8 2.3 convolution_convert_fusion
  33.1 2.3 convolution_convert_fusion.1
  36.7 11.0 %all-to-all-start = ((bf16[32,16,896]{2,1,0:T(8,128)(2,1)}), bf16[32,16,896]{2,1,0:T(8,128)(2,1)S(1)}, u32[]{:S(2)}, u32[]{:S(2)}) async-start(bf16[32,16,896]{2,1,0:T(8,128)(2,1)} %bitcast.331), calls=%async_computation | async-start | bytes 1835008 | tf_op jit(solution)/shard_map/all_to_all | solution.py:55
  47.7 3.9 copy.169
  51.6 21.3 %all-to-all-done.state_ref = bf16[32,16,896]{2,1,0:T(8,128)(2,1)S(1)} async-done(((bf16[32,16,896]{2,1,0:T(8,128)(2,1)}), bf16[32,16,896]{2,1,0:T(8,128)(2,1)S(1)}, u32[]{:S(2)}, u32[]{:S(2)}) %all-to-all-start) | async-done | bytes 917536 | tf_op jit(solution)/shard_map/all_to_all | solution.py:55
  72.9 5.5 %all-to-all-start.3 = ((bf16[128,32,224]{0,2,1:T(8,128)(2,1)}), bf16[128,32,224]{0,2,1:T(8,128)(2,1)}, u32[]{:S(2)}, u32[]{:S(2)}) async-start(bf16[128,32,224]{0,2,1:T(8,128)(2,1)} %bitcast.321), calls=%async_computation.3 | async-start | bytes 3670016 | tf_op jit(solution)/shard_map/all_to_all | solution.py:176
  78.4 3.9 copy.171
  82.3 39.5 %all-to-all-done.3 = bf16[128,32,224]{0,2,1:T(8,128)(2,1)} async-done(((bf16[128,32,224]{0,2,1:T(8,128)(2,1)}), bf16[128,32,224]{0,2,1:T(8,128)(2,1)}, u32[]{:S(2)}, u32[]{:S(2)}) %all-to-all-start.3) | async-done | bytes 1835040 | tf_op jit(solution)/shard_map/all_to_all | solution.py:176
  121.8 6.0 %all-to-all-start.4 = ((bf16[128,32,224]{0,2,1:T(8,128)(2,1)}), bf16[128,32,224]{0,2,1:T(8,128)(2,1)}, u32[]{:S(2)}, u32[]{:S(2)}) async-start(bf16[128,32,224]{0,2,1:T(8,128)(2,1)} %bitcast.320), calls=%async_computation.4 | async-start | bytes 3670016 | tf_op jit(solution)/shard_map/all_to_all | solution.py:177
  127.8 70.8 %all-gather = f32[32,1,112]{2,1,0:T(1,128)S(1)} all-gather(f32[1,1,112]{2,1,0:T(1,128)S(1)} %get-tuple-element.28), channel_id=1, replica_groups=mesh['dp'=8,'ctx'=32] {'ctx'}, dimensions={0}, use_global_device_ids=true | all-gather | bytes 14784 | tf_op jit(solution)/shard_map/all_gather | solution.py:51
  199.2 2.0 broadcast_in_dim.55
  201.3 5.3 %copy.164 = f32[128,7168]{1,0:T(8,128)} copy(f32[128,7168]{0,1:T(8,128)} %bitcast.315) | data formatting | bytes 7340032 | tf_op jit(solution)/shard_map/reshape | solution.py:173
  207.3 5.8 %reshape.470 = f32[128,2,3584]{2,1,0:T(2,128)} reshape(bf16[128,7168]{1,0:T(8,128)(2,1)} %param.12) | data formatting | bytes 5505024 | tf_op jit(solution)/shard_map/reshape | solution.py:68
  214.3 1.4 slice.195
  215.8 3.9 copy.151
  219.9 10.5 %fusion.1 = f32[2,56,64,128]{3,2,1,0:T(8,128)} fusion(bf16[128,2,56,64]{0,3,2,1:T(8,128)(2,1)} %bitcast.337, f32[2,56,128]{2,1,0:T(8,128)S(1)} %bitcast.348, f32[2,56,128]{2,1,0:T(8,128)S(1)} %bitcast.349, f32[2,128,128]{2,1,0:T(8,128)S(1)} %fusion.145, pred[128,128]{1,0:T(8,128)(4,1)S(1)} %iota_compare_fusion.8), kind=kOutput, calls=%fused_computation.9 | convolution fusion | flops 1416626176 | bytes 5767168 | tf_op jit(solution)/shard_map/gkts,sgkp->tgkp/dot_general | solution.py:158
  230.5 5.3 %copy.157 = f32[128,7168]{1,0:T(8,128)} copy(f32[128,7168]{0,1:T(8,128)} %bitcast.329) | data formatting | bytes 7340032 | tf_op jit(solution)/shard_map/reshape | solution.py:159
  236.9 2.8 slice_bitcast_fusion.10
  239.7 6.6 %all-to-all-start.1 = ((bf16[32,16,896]{2,1,0:T(8,128)(2,1)}), bf16[32,16,896]{2,1,0:T(8,128)(2,1)S(1)}, u32[]{:S(2)}, u32[]{:S(2)}) async-start(bf16[32,16,896]{2,1,0:T(8,128)(2,1)} %shard_map.122), calls=%async_computation.1 | async-start | bytes 1835008 | tf_op jit(solution)/shard_map/all_to_all | solution.py:61
  246.3 3.4 fusion.138
  249.8 1.1 slice.215
  250.9 1.2 copy.178
  252.1 2.0 fusion.36
  254.1 2.3 fusion.139
  257.0 2.5 fusion.137
  259.6 2.2 fusion.140
  261.8 2.1 copy-done.10
  266.6 1.2 copy-done.1
  267.7 2.8 fusion.23
  270.5 6.1 %reshape.469 = f32[128,2,3584]{2,1,0:T(2,128)} reshape(f32[128,7168]{1,0:T(8,128)} %fusion.23) | data formatting | bytes 7340032 | tf_op jit(solution)/shard_map/reshape | solution.py:69
  276.6 6.9 %multiply_reduce_fusion = f32[128,2]{1,0:T(8,128)S(1)} fusion(f32[128,2,3584]{2,1,0:T(2,128)} %reshape.469, f32[128,2,3584]{2,1,0:T(2,128)} %reshape.470), kind=kLoop, calls=%fused_computation.57 | loop fusion | flops 6422272 | bytes 7341056 | tf_op jit(solution)/shard_map/reduce_sum | solution.py:70
  285.2 1.4 copy-done
  287.2 1.3 multiply_convert_fusion.1
  288.5 2.3 copy.167
  290.8 10.2 %all-to-all-start.2 = ((bf16[128,32,224]{0,2,1:T(8,128)(2,1)}), bf16[128,32,224]{0,2,1:T(8,128)(2,1)}, u32[]{:S(2)}, u32[]{:S(2)}) async-start(bf16[128,32,224]{0,2,1:T(8,128)(2,1)} %bitcast.22), calls=%async_computation.2 | async-start | bytes 3670016 | tf_op jit(solution)/shard_map/all_to_all | solution.py:178
  301.2 2.4 fusion.141
  304.5 1.5 copy-done.9
  305.9 2.7 fusion.142
  309.7 1.6 copy-done.8
  311.3 3.0 fusion.143
  315.4 1.9 copy-done.5
  317.3 3.3 fusion.144
  320.6 3.2 copy-done.4
  323.8 1.3 fusion
  325.1 10.3 %all-to-all-done.2 = bf16[128,32,224]{0,2,1:T(8,128)(2,1)} async-done(((bf16[128,32,224]{0,2,1:T(8,128)(2,1)}), bf16[128,32,224]{0,2,1:T(8,128)(2,1)}, u32[]{:S(2)}, u32[]{:S(2)}) %all-to-all-start.2) | async-done | bytes 1835040 | tf_op jit(solution)/shard_map/all_to_all | solution.py:178
  335.4 1.1 slice.213
  336.5 2.0 fusion.66
  338.8 3.2 fusion.84
  342.1 1.7 fusion.86
  344.3 3.4 fusion.68
  347.8 3.4 fusion.82
  351.2 3.7 fusion.90
  355.0 4.0 fusion.78
  359.0 4.1 %fusion.72 = bf16[4096,224]{0,1:T(8,128)(2,1)} fusion(bf16[4096,224]{0,1:T(8,128)(2,1)} %fusion.78, f32[512,4096]{1,0:T(8,128)S(1)} %bitcast.319, f32[512]{0:T(512)S(1)} %fusion, f32[512]{0:T(512)S(1)} %get-tuple-element.43, bf16[128,32,224]{0,2,1:T(8,128)(2,1)} %all-to-all-done.2), kind=kOutput, calls=%fused_computation.114 | convolution fusion | flops 945930240 | bytes 10457088 | tf_op jit(solution)/shard_map/hqk,khd->qhd/dot_general | solution.py:102
  363.1 1.8 copy_bitcast_fusion
  364.9 40.5 %all_to_all.77 = bf16[32,128,224]{1,2,0:T(8,128)(2,1)} all-to-all(bf16[32,128,224]{1,2,0:T(8,128)(2,1)S(1)} %copy_bitcast_fusion), channel_id=1, replica_groups=mesh['dp'=8,'ctx'=32] {'ctx'}, dimensions={0} | all-to-all | bytes 3670016 | tf_op jit(solution)/shard_map/all_to_all | solution.py:181
  405.4 3.9 copy.195
  (117 shorter events, 19.3 us)
Async XLA Ops:
  1.6 19.2 %collective-permute-start = (bf16[3,7424]{1,0:T(4,128)(2,1)S(1)}, bf16[3,7424]{1,0:T(4,128)(2,1)S(1)}, u32[]{:S(2)}, u32[]{:S(2)}) collective-permute-start(bf16[3,7424]{1,0:T(4,128)(2,1)S(1)} %slice.150), channel_id=1, source_target_pairs={{0,1},{1,2},{2,3},{3,4},{4,5},{5,6},{6,7},{7,8},{8,9},{9,10},{10,1... | collective-permute-start | bytes 133640 | tf_op jit(solution)/shard_map/ppermute | solution.py:30
  15.5 5.3 %copy-start.22 = (f32[7424]{0:T(1024)S(1)}, f32[7424]{0:T(1024)}, u32[]{:S(2)}) copy-start(f32[7424]{0:T(1024)} %param.18) | copy-start | bytes 89092
  20.8 7.7 %copy-start.3 = (f32[128,7168]{1,0:T(8,128)S(1)}, f32[128,7168]{1,0:T(8,128)}, u32[]{:S(2)}) copy-start(f32[128,7168]{1,0:T(8,128)} %copy.159) | copy-start | bytes 11010052
  36.7 36.2 %all-to-all-start = ((bf16[32,16,896]{2,1,0:T(8,128)(2,1)}), bf16[32,16,896]{2,1,0:T(8,128)(2,1)S(1)}, u32[]{:S(2)}, u32[]{:S(2)}) async-start(bf16[32,16,896]{2,1,0:T(8,128)(2,1)} %bitcast.331), calls=%async_computation | async-start | bytes 1835008 | tf_op jit(solution)/shard_map/all_to_all | solution.py:55
  72.9 48.9 %all-to-all-start.3 = ((bf16[128,32,224]{0,2,1:T(8,128)(2,1)}), bf16[128,32,224]{0,2,1:T(8,128)(2,1)}, u32[]{:S(2)}, u32[]{:S(2)}) async-start(bf16[128,32,224]{0,2,1:T(8,128)(2,1)} %bitcast.321), calls=%async_computation.3 | async-start | bytes 3670016 | tf_op jit(solution)/shard_map/all_to_all | solution.py:176
  121.8 118.0 %all-to-all-start.4 = ((bf16[128,32,224]{0,2,1:T(8,128)(2,1)}), bf16[128,32,224]{0,2,1:T(8,128)(2,1)}, u32[]{:S(2)}, u32[]{:S(2)}) async-start(bf16[128,32,224]{0,2,1:T(8,128)(2,1)} %bitcast.320), calls=%async_computation.4 | async-start | bytes 3670016 | tf_op jit(solution)/shard_map/all_to_all | solution.py:177
  201.3 5.3 %copy-start.26 = (f32[112]{0:T(128)S(1)}, f32[112]{0:T(128)}, u32[]{:S(2)}) copy-start(f32[112]{0:T(128)} %param.16) | copy-start | bytes 1348
  239.7 24.8 %all-to-all-start.1 = ((bf16[32,16,896]{2,1,0:T(8,128)(2,1)}), bf16[32,16,896]{2,1,0:T(8,128)(2,1)S(1)}, u32[]{:S(2)}, u32[]{:S(2)}) async-start(bf16[32,16,896]{2,1,0:T(8,128)(2,1)} %shard_map.122), calls=%async_computation.1 | async-start | bytes 1835008 | tf_op jit(solution)/shard_map/all_to_all | solution.py:61
  254.1 2.9 copy-start.20
  256.4 5.3 %copy-start.12 = (f32[512,1536]{1,0:T(8,128)}, f32[512,1536]{1,0:T(8,128)S(1)}, u32[]{:S(2)}) copy-start(f32[512,1536]{1,0:T(8,128)S(1)} %get-tuple-element.34) | copy-start | bytes 9437188
  256.4 3.1 copy-start.19
  256.4 3.1 copy-start.24
  261.8 2.1 copy-start.10
  264.5 2.0 copy-start.2
  264.7 3.0 copy-start.1
  264.7 3.0 copy-start.21
  284.5 2.0 copy-start
  284.5 2.6 copy-start.7
  284.6 2.6 copy-start.23
  288.4 2.3 copy-start.6
  288.4 12.5 %copy-start.14 = (f32[512,512]{0,1:T(8,128)S(1)}, f32[512,512]{0,1:T(8,128)}, u32[]{:S(2)}) copy-start(f32[512,512]{0,1:T(8,128)} %get-tuple-element.30) | copy-start | bytes 3145732
  288.5 12.7 %copy-start.18 = (bf16[4,28,8,128]{3,2,1,0:T(8,128)(2,1)S(1)}, bf16[4,28,8,128]{3,2,1,0:T(8,128)(2,1)}, u32[]{:S(2)}) copy-start(bf16[4,28,8,128]{3,2,1,0:T(8,128)(2,1)} %get-tuple-element.19) | copy-start | bytes 688132
  290.8 44.6 %all-to-all-start.2 = ((bf16[128,32,224]{0,2,1:T(8,128)(2,1)}), bf16[128,32,224]{0,2,1:T(8,128)(2,1)}, u32[]{:S(2)}, u32[]{:S(2)}) async-start(bf16[128,32,224]{0,2,1:T(8,128)(2,1)} %bitcast.22), calls=%async_computation.2 | async-start | bytes 3670016 | tf_op jit(solution)/shard_map/all_to_all | solution.py:178
  303.6 2.3 copy-start.9
  303.6 2.3 copy-start.17
  308.7 2.6 copy-start.8
  308.7 2.6 copy-start.16
  314.3 3.0 copy-start.5
  314.3 3.0 copy-start.15
  320.6 3.2 copy-start.4
  335.4 3.4 copy-start.25
  338.8 3.2 copy-start.13
  342.1 2.3 copy-start.11
  342.1 5.7 %slice-start.6 = ((s8[5242880]{0:T(1024)(128)(4,1)}), s8[4194304]{0:T(1024)(128)(4,1)S(1)}, s32[]{:S(2)}) async-start(s8[5242880]{0:T(1024)(128)(4,1)} %bitcast.327), calls=%async_computation.12 | async-start | bytes 8388608
  344.3 3.5 slice-start.7
  344.3 6.9 %slice-start.4 = ((s8[6291456]{0:T(1024)(128)(4,1)}), s8[4194304]{0:T(1024)(128)(4,1)S(1)}, s32[]{:S(2)}) async-start(s8[6291456]{0:T(1024)(128)(4,1)} %bitcast.325), calls=%async_computation.10 | async-start | bytes 8388608
  347.8 3.4 slice-start.5
  347.8 7.2 %slice-start.2 = ((s8[7340032]{0:T(1024)(128)(4,1)}), s8[4194304]{0:T(1024)(128)(4,1)S(1)}, s32[]{:S(2)}) async-start(s8[7340032]{0:T(1024)(128)(4,1)} %bitcast.323), calls=%async_computation.8 | async-start | bytes 8388608
  351.2 3.7 slice-start.3
  351.2 7.7 %slice-start = ((s8[8388608]{0:T(1024)(128)(4,1)}), s8[4194304]{0:T(1024)(128)(4,1)S(1)}, s32[]{:S(2)}) async-start(s8[8388608]{0:T(1024)(128)(4,1)} %bitcast.318), calls=%async_computation.6 | async-start | bytes 8388608
  355.0 4.0 slice-start.1

commit v2 on v1

v2 whole, which is shorter than its diff:
```python
import functools
import math

import jax
import jax.numpy as jnp
from jax import lax
from jax.experimental import pallas as pl
from jax.experimental.pallas import tpu as pltpu
from jax.sharding import PartitionSpec as P

HEADS = 112
HEAD_DIM = 64
STATE = 64
GROUPS = 2
CONV = 4
ATT_DIM = 224
INNER = HEADS * HEAD_DIM
SHARE = INNER // GROUPS

ROW_PARTS = 4
COL_PARTS = 8
PART_ROWS = STATE // ROW_PARTS
PART_COLS = INNER // COL_PARTS
LANES = 128
PART_TILES = PART_COLS // LANES
PART_HEADS = PART_COLS // HEAD_DIM
STATE_ROWS = PART_TILES * PART_ROWS

QUERY_BLOCK = 512
KEY_BLOCK = 1024

dt_cap = 3.0
eps = 1e-05
HIGHEST = lax.Precision.HIGHEST
VMEM_LIMIT = 56 * 1024 * 1024
PARAMS = pltpu.CompilerParams(vmem_limit_bytes=VMEM_LIMIT)


def shifted(array, axis, by):
    size = lax.axis_size(axis)
    pairs = [(i, i + by) for i in range(size) if 0 <= i + by < size]
    return lax.ppermute(array, axis, pairs)


def exchanged(array):
    return lax.all_to_all(array, "ctx", 0, 0, tiled=True)


def convolve(padded, conv_weight, conv_bias, row_count):
    total = conv_bias[None, :] + conv_weight[0][None, :] * padded[0:row_count]
    for tap_index in range(1, conv_weight.shape[0]):
        total = total + conv_weight[tap_index][None, :] * padded[tap_index : tap_index + row_count]
    return jax.nn.silu(total).astype(jnp.bfloat16)


def per_channel(by_head):
    return jnp.repeat(by_head, HEAD_DIM, axis=-1)


def turn_kernel(query_ref, key_ref, out_ref):
    heads = out_ref.shape[0]
    for source, offset in ((query_ref, 0), (key_ref, ATT_DIM)):
        turned = source[...].T
        for h in range(heads):
            out_ref[h, offset : offset + ATT_DIM] = turned[h * ATT_DIM : (h + 1) * ATT_DIM]


def turned_rows(queries, key_rows):
    rows, width = queries.shape
    heads = width // ATT_DIM
    steps = 8
    per_step = heads // steps
    block = pl.BlockSpec((rows, width // steps), lambda i: (0, i))
    return pl.pallas_call(
        turn_kernel,
        grid=(steps,),
        in_specs=[block, block],
        out_specs=pl.BlockSpec((per_step, 2 * ATT_DIM, rows), lambda i: (i, 0, 0)),
        out_shape=jax.ShapeDtypeStruct((heads, 2 * ATT_DIM, rows), queries.dtype),
        compiler_params=PARAMS,
    )(queries, key_rows)


def scan_kernel(recv_ref, out_ref):
    blocks = recv_ref.shape[0]
    lane = lax.broadcasted_iota(jnp.int32, (LANES, PART_COLS), 0)
    column = lax.broadcasted_iota(jnp.int32, (LANES, PART_COLS), 1)
    spread = (column // HEAD_DIM == lane).astype(jnp.float32).astype(jnp.bfloat16)
    pieces = recv_ref[:, STATE_ROWS:].reshape(blocks * PART_ROWS, LANES)
    decays = jnp.dot(pieces, spread, preferred_element_type=jnp.float32)
    state = [jnp.zeros((PART_ROWS, LANES), jnp.float32) for _ in range(PART_TILES)]
    for block in range(blocks):
        decay = jnp.sum(
            decays[block * PART_ROWS : block * PART_ROWS + 8], axis=0, keepdims=True
        )
        for tile in range(PART_TILES):
            rows = slice(tile * PART_ROWS, (tile + 1) * PART_ROWS)
            out_ref[block, rows] = state[tile].astype(jnp.bfloat16)
            added = recv_ref[block, rows].astype(jnp.float32)
            state[tile] = (
                state[tile] * decay[:, tile * LANES : (tile + 1) * LANES] + added
            )


def packed_state(local_state, block_decay):
    parts = local_state.astype(jnp.bfloat16).reshape(
        ROW_PARTS, PART_ROWS, COL_PARTS, PART_TILES, LANES
    )
    parts = parts.transpose(0, 2, 3, 1, 4).reshape(-1, STATE_ROWS, LANES)
    high = lax.reduce_precision(block_decay, 8, 7)
    middle = lax.reduce_precision(block_decay - high, 8, 7)
    low = lax.reduce_precision(block_decay - high - middle, 8, 7)
    pieces = jnp.stack([high, middle, low]).astype(jnp.bfloat16)
    pieces = pieces.reshape(3, COL_PARTS, PART_HEADS).transpose(1, 0, 2)
    pieces = jnp.pad(pieces, ((0, 0), (0, PART_ROWS - 3), (0, LANES - PART_HEADS)))
    pieces = jnp.tile(pieces, (ROW_PARTS, 1, 1))
    return jnp.concatenate([parts, pieces], axis=1)


def scanned(received):
    return pl.pallas_call(
        scan_kernel,
        out_shape=jax.ShapeDtypeStruct((received.shape[0], STATE_ROWS, LANES), jnp.bfloat16),
        compiler_params=PARAMS,
    )(received)


def norm_kernel(readout_ref, state_ref, base_ref, factor_ref, gain_ref, out_ref, turned_ref, held):
    group, chunk = pl.program_id(0), pl.program_id(1)
    chunks = held.shape[0]
    readout = jnp.where(group == 0, readout_ref[:, :STATE], readout_ref[:, STATE:])
    tiles = []
    for tile in range(PART_TILES):
        rows = slice(tile * PART_ROWS, (tile + 1) * PART_ROWS)
        tiles.append(
            jnp.concatenate([state_ref[part, 0, rows] for part in range(ROW_PARTS)], axis=0)
        )
    state = jnp.concatenate(tiles, axis=1)
    across = jnp.dot(readout, state, preferred_element_type=jnp.float32)
    held[chunk] = base_ref[...] + across * factor_ref[...]

    @pl.when(chunk == chunks - 1)
    def _():
        total = jnp.zeros((held.shape[1], 1), jnp.float32)
        for c in range(chunks):
            total = total + jnp.sum(held[c] * held[c], axis=1, keepdims=True)
        scale = lax.rsqrt(total / SHARE + eps)
        per_chunk = PART_COLS // ATT_DIM
        for c in range(chunks):
            columns = slice(c * PART_COLS, (c + 1) * PART_COLS)
            normed = (held[c] * scale * gain_ref[:, columns]).astype(jnp.bfloat16)
            out_ref[:, columns] = normed
            turned = normed.T
            for h in range(per_chunk):
                turned_ref[c * per_chunk + h] = turned[h * ATT_DIM : (h + 1) * ATT_DIM]


def normed_output(readout, state_in, base, factor, norm_gain):
    rows = base.shape[0]
    chunks = COL_PARTS // GROUPS
    state_in = state_in.reshape(ROW_PARTS, COL_PARTS, STATE_ROWS, LANES)
    wide = pl.BlockSpec((rows, PART_COLS), lambda g, c: (0, g * chunks + c))
    heads = INNER // ATT_DIM // GROUPS
    return pl.pallas_call(
        norm_kernel,
        grid=(GROUPS, chunks),
        in_specs=[
            pl.BlockSpec((rows, GROUPS * STATE), lambda g, c: (0, 0)),
            pl.BlockSpec(
                (ROW_PARTS, 1, STATE_ROWS, LANES), lambda g, c: (0, g * chunks + c, 0, 0)
            ),
            wide,
            wide,
            pl.BlockSpec((1, SHARE), lambda g, c: (0, g)),
        ],
        out_specs=[
            pl.BlockSpec((rows, SHARE), lambda g, c: (0, g)),
            pl.BlockSpec((heads, ATT_DIM, rows), lambda g, c: (g, 0, 0)),
        ],
        out_shape=[
            jax.ShapeDtypeStruct((rows, INNER), jnp.bfloat16),
            jax.ShapeDtypeStruct((GROUPS * heads, ATT_DIM, rows), jnp.bfloat16),
        ],
        scratch_shapes=[pltpu.VMEM((chunks, rows, PART_COLS), jnp.float32)],
        compiler_params=PARAMS,
    )(readout, state_in, base, factor, norm_gain.reshape(1, INNER))


def weight_kernel(query_ref, key_ref, out_ref, keys, scores):
    step = pl.program_id(0)
    sources, _, rows = key_ref.shape

    @pl.when(step == 0)
    def _():
        for source in range(sources):
            keys[source * rows : (source + 1) * rows] = key_ref[source, ATT_DIM:].T

    queries = jnp.concatenate([query_ref[b] for b in range(query_ref.shape[0])], axis=1)
    chunks = (step + KEY_BLOCK // QUERY_BLOCK) // (KEY_BLOCK // QUERY_BLOCK)
    score_scale = 1.0 / math.sqrt(ATT_DIM)

    def raw(chunk):
        part = keys[pl.ds(pl.multiple_of(chunk * KEY_BLOCK, KEY_BLOCK), KEY_BLOCK)]
        return jnp.dot(part, queries, preferred_element_type=jnp.float32) * score_scale

    def slots(chunk):
        return pl.ds(pl.multiple_of(chunk * KEY_BLOCK, KEY_BLOCK), KEY_BLOCK)

    def first(chunk, top):
        values = raw(chunk)
        scores[slots(chunk)] = values
        return jnp.maximum(top, jnp.max(values.reshape(-1, 8, QUERY_BLOCK), axis=0))

    top = jnp.full((8, QUERY_BLOCK), -jnp.inf, jnp.float32)
    top = lax.fori_loop(0, chunks - 1, first, top)
    last = chunks - 1
    key_pos = last * KEY_BLOCK + lax.broadcasted_iota(jnp.int32, (KEY_BLOCK, QUERY_BLOCK), 0)
    query_pos = step * QUERY_BLOCK + lax.broadcasted_iota(
        jnp.int32, (KEY_BLOCK, QUERY_BLOCK), 1
    )
    values = jnp.where(key_pos <= query_pos, raw(last), -jnp.inf)
    scores[slots(last)] = values
    top = jnp.maximum(top, jnp.max(values.reshape(-1, 8, QUERY_BLOCK), axis=0))
    top = jnp.max(top, axis=0, keepdims=True)

    def second(chunk, total):
        values = jnp.exp(scores[slots(chunk)] - top)
        scores[slots(chunk)] = values
        return total + jnp.sum(values.reshape(-1, 8, QUERY_BLOCK), axis=0)

    total = lax.fori_loop(0, chunks, second, jnp.zeros((8, QUERY_BLOCK), jnp.float32))
    inverse = 1.0 / jnp.sum(total, axis=0, keepdims=True)

    def third(chunk, carry):
        out_ref[0, slots(chunk)] = (scores[slots(chunk)] * inverse).astype(jnp.bfloat16)
        return carry

    lax.fori_loop(0, chunks, third, 0)


def attention_weights(received):
    sources, _, rows = received.shape
    total = sources * rows
    steps = total // QUERY_BLOCK
    per_step = QUERY_BLOCK // rows
    return pl.pallas_call(
        weight_kernel,
        grid=(steps,),
        in_specs=[
            pl.BlockSpec((per_step, ATT_DIM, rows), lambda i: (i, 0, 0)),
            pl.BlockSpec((sources, 2 * ATT_DIM, rows), lambda i: (0, 0, 0)),
        ],
        out_specs=pl.BlockSpec((1, total, QUERY_BLOCK), lambda i: (i, 0, 0)),
        out_shape=jax.ShapeDtypeStruct((steps, total, QUERY_BLOCK), jnp.bfloat16),
        scratch_shapes=[
            pltpu.VMEM((total, ATT_DIM), jnp.bfloat16),
            pltpu.VMEM((total, QUERY_BLOCK), jnp.float32),
        ],
        compiler_params=PARAMS,
    )(received, received)


def mix_kernel(block_ref, chunk_ref, value_ref, weight_ref, out_ref, total):
    step = pl.program_id(0)
    chunk = chunk_ref[step]
    per_chunk = KEY_BLOCK // value_ref.shape[2]
    values = jnp.concatenate([value_ref[chunk * per_chunk + b] for b in range(per_chunk)], axis=1)
    product = jnp.dot(values, weight_ref[0], preferred_element_type=jnp.float32)

    @pl.when(chunk == 0)
    def _():
        total[...] = product

    @pl.when(chunk > 0)
    def _():
        total[...] += product

    @pl.when(chunk == block_ref[step] // (KEY_BLOCK // QUERY_BLOCK))
    def _():
        rows = out_ref.shape[2]
        for b in range(out_ref.shape[0]):
            out_ref[b] = total[:, b * rows : (b + 1) * rows].astype(jnp.bfloat16)


def mixed(weights, values):
    steps, total, _ = weights.shape
    sources, _, rows = values.shape
    pairs = [
        (i, c) for i in range(steps) for c in range(i * QUERY_BLOCK // KEY_BLOCK + 1)
    ]
    blocks = jnp.array([i for i, _ in pairs], jnp.int32)
    chunks = jnp.array([c for _, c in pairs], jnp.int32)
    return pl.pallas_call(
        mix_kernel,
        grid_spec=pltpu.PrefetchScalarGridSpec(
            num_scalar_prefetch=2,
            grid=(len(pairs),),
            in_specs=[
                pl.BlockSpec((sources, ATT_DIM, rows), lambda s, b, c: (0, 0, 0)),
                pl.BlockSpec((1, KEY_BLOCK, QUERY_BLOCK), lambda s, b, c: (b[s], c[s], 0)),
            ],
            out_specs=pl.BlockSpec(
                (QUERY_BLOCK // rows, ATT_DIM, rows), lambda s, b, c: (b[s], 0, 0)
            ),
            scratch_shapes=[pltpu.VMEM((ATT_DIM, QUERY_BLOCK), jnp.float32)],
        ),
        out_shape=jax.ShapeDtypeStruct((sources, ATT_DIM, rows), jnp.bfloat16),
        compiler_params=PARAMS,
    )(blocks, chunks, values, weights)


def local(
    conv_input,
    gate_input,
    step_raw,
    step_bias,
    decay_log,
    skip_weight,
    conv_weight,
    conv_bias,
    norm_gain,
    queries,
    key_rows,
):
    row_count = conv_input.shape[0]
    share = HEADS // GROUPS
    before = shifted(conv_input[row_count - (CONV - 1) :], "ctx", 1)
    received = exchanged(turned_rows(queries, key_rows))

    padded = jnp.concatenate([before.astype(jnp.float32), conv_input.astype(jnp.float32)], axis=0)
    inputs = convolve(padded, conv_weight, conv_bias, row_count)
    step_rates = jnp.minimum(jax.nn.softplus(step_raw + step_bias[None, :]), dt_cap)
    decay_rate = -jnp.exp(decay_log)
    running = jnp.cumsum(step_rates * decay_rate[None], axis=0)
    values = inputs[:, :INNER].astype(jnp.float32)
    writes = inputs[:, INNER : INNER + GROUPS * STATE].reshape(row_count, GROUPS, STATE)
    readout_low = inputs[:, INNER + GROUPS * STATE :]
    readout = readout_low.reshape(row_count, GROUPS, STATE)
    carry_weight = jnp.exp(running[-1][None] - running) * step_rates
    weighted = values * per_channel(carry_weight)
    local_state = jnp.concatenate(
        [
            jnp.einsum(
                "sn,sc->nc",
                writes[:, g].astype(jnp.float32),
                weighted[:, g * SHARE : (g + 1) * SHARE],
                precision=HIGHEST,
            )
            for g in range(GROUPS)
        ],
        axis=1,
    )
    parts = packed_state(local_state, jnp.exp(running[-1]))
    received, parts = lax.optimization_barrier((received, parts))
    state_in = exchanged(scanned(exchanged(parts)))

    running_heads = running.T.reshape(GROUPS, share, row_count)
    rates_heads = step_rates.T.reshape(GROUPS, share, row_count)
    positions = jnp.arange(row_count, dtype=jnp.int32)
    causal = (positions[:, None] >= positions[None, :])[None, None]
    spread = running_heads[:, :, :, None] - running_heads[:, :, None, :]
    fading = jnp.exp(jnp.where(causal, spread, -jnp.inf))
    intersection = jnp.einsum("tgn,sgn->gts", readout, writes, preferred_element_type=jnp.float32)
    mixing = intersection[:, None] * fading * rates_heads[:, :, None, :]
    grouped = values.reshape(row_count, GROUPS, share, HEAD_DIM)
    inside = jnp.einsum("gkts,sgkp->tgkp", mixing, grouped, precision=HIGHEST)
    gate = jax.nn.silu(gate_input.astype(jnp.float32))
    base = (inside.reshape(row_count, INNER) + per_channel(skip_weight)[None] * values) * gate
    factor = per_channel(jnp.exp(running)) * gate

    mamba_out, turned_out = normed_output(readout_low, state_in, base, factor, norm_gain)
    weights = attention_weights(received)
    attended_heads = mixed(weights, exchanged(turned_out))
    attended = exchanged(attended_heads)
    attended = attended.transpose(2, 0, 1).reshape(row_count, INNER)
    return (mamba_out, attended)


def solution(mesh):
    rows = P(("dp", "ctx"), None)
    placed = (rows, rows, rows, P(), P(), P(), P(), P(), P(), rows, rows)
    return jax.shard_map(
        local, mesh=mesh, in_specs=placed, out_specs=(rows, rows), check_vma=False
    )
```

time: 417 us -> 306 us (0.73); the launches traced: 409 us -> 304 us
  Pallas kernels: 1.13 us -> 63.1 us
  matrix products: 63.7 us -> 12.4 us
  local copies, waits for them, and re-layouts: 82.6 us -> 34 us
  waiting for transfers between devices: 71.1 us -> 43.6 us
  starting transfers between devices: 42.7 us -> 20.1 us
  other arithmetic: 35.8 us -> 17.6 us
    all_to_all x1 -> x3, blocking collectives: 40.5 us -> 113 us  [exchanged(): return lax.all_to_all(array, 'ctx', 0, 0, tiled=True)]
    all_gather x1 -> x0, blocking collectives: 70.8 us -> none  [states_before(): all_decay = lax.all_gather(block_decay, 'ctx')]
    pallas_call x1 -> x5, Pallas kernels: 1.13 us -> 63.1 us  [the longest x1 23.1 us: attention_weights(): pl.pallas_call(weight_kernel, grid=(steps,), in_specs=[pl.BlockSpec((per_...]
    dot_general x18 -> x0, matrix products: 48.3 us -> none  [the longest x8 25.6 us: attend(): jnp.einsum('hqk,khd->qhd', weights, value_all[:block_stop], preferred_ele...]
    all_to_all x5 -> x2, waiting for transfers between devices: 71.1 us -> 43.6 us  [exchanged(): return lax.all_to_all(array, 'ctx', 0, 0, tiled=True)]
    unnamed x78 -> x21, local copies, waits for them, and re-layouts: 31.2 us -> 4.23 us
    all_to_all x5 -> x2, starting transfers between devices: 39.3 us -> 16.7 us  [exchanged(): return lax.all_to_all(array, 'ctx', 0, 0, tiled=True)]
    reduce_sum x9 -> x0, other arithmetic: 14.7 us -> none  [the longest x8 7.74 us: attend(): jnp.sum(exponent, axis=2, keepdims=True)]
  transfers between devices with their start and end apart: 6 -> 3, of which waited for: 3 -> 2; matrix products, arithmetic and copies ran while one was open for 23% -> 19% of each run, Pallas kernels for 0% -> 10%
where the time goes in v2:
time: 306 us; the launch traced here: 304 us
  blocking collectives  113 us (37%)
  Pallas kernels  63.1 us (21%)
  waiting for transfers between devices  43.6 us (14%)
  local copies, waits for them, and re-layouts  34 us (11%)
  starting transfers between devices  20.1 us (7%)
  other arithmetic  17.6 us (6%)
  matrix products  12.4 us (4%)
    all_to_all x3, blocking collectives, exchanged(): return lax.all_to_all(array, 'ctx', 0, 0, tiled=True)  113 us
    all_to_all x2, waiting for transfers between devices, exchanged(): return lax.all_to_all(array, 'ctx', 0, 0, tiled=True)  43.6 us
    pallas_call x1, Pallas kernels, attention_weights(): pl.pallas_call(weight_kernel, grid=(steps,), in_specs=[pl.BlockSpec((per_...  23.1 us
    pallas_call x1, Pallas kernels, mixed(): pl.pallas_call(mix_kernel, grid_spec=pltpu.PrefetchScalarGridSpec(num_sca...  20.8 us
    all_to_all x2, starting transfers between devices, exchanged(): return lax.all_to_all(array, 'ctx', 0, 0, tiled=True)  16.7 us
    dot_general x1, matrix products, local(): inside = jnp.einsum('gkts,sgkp->tgkp', mixing, grouped, precision=HIGHEST)  10.6 us
    reshape x2, local copies, waits for them, and re-layouts, per_channel(): return jnp.repeat(by_head, HEAD_DIM, axis=-1)  10.5 us
    pallas_call x1, Pallas kernels, normed_output(): pl.pallas_call(norm_kernel, grid=(GROUPS, chunks), in_specs=[pl.BlockSpec...  9.41 us
  transfers between devices with their start and end apart: 3, of which 2 were waited for; matrix products, arithmetic and copies ran while one was open for 19% of the time, Pallas kernels for 10%

profile of v2, /device:TPU:16, one launch (start us, length us, event | category | flops | bytes accessed | tf_op | source)
XLA Modules:
  0.0 304.5 jit_solution(4482703116201208743)
XLA Ops:
  0.6 0.9 slice.50
  1.6 3.4 %collective-permute-start = (bf16[3,7424]{1,0:T(4,128)(2,1)S(1)}, bf16[3,7424]{1,0:T(4,128)(2,1)S(1)}, u32[]{:S(2)}, u32[]{:S(2)}) collective-permute-start(bf16[3,7424]{1,0:T(4,128)(2,1)S(1)} %slice.50), channel_id=1, source_target_pairs={{0,1},{1,2},{2,3},{3,4},{4,5},{5,6},{6,7},{7,8},{8,9},{9,10},{10,1... | collective-permute-start | bytes 133640 | tf_op jit(solution)/shard_map/ppermute | solution.py:42
  5.0 7.1 %shard_map.140 = bf16[32,448,128]{2,1,0:T(8,128)(2,1)} custom-call(bf16[128,7168]{1,0:T(8,128)(2,1)} %query_ref.1, bf16[128,7168]{1,0:T(8,128)(2,1)} %key_ref.1), custom_call_target="tpu_custom_call" | custom-call | tf_op jit(solution)/shard_map/pallas_call | solution.py:74
  12.1 0.0 copy-start.8
  12.1 0.0 copy-start.4
  12.1 0.0 copy-start.3
  12.1 0.0 copy-start.1
  12.1 11.3 %all-to-all-start = ((bf16[32,448,128]{2,1,0:T(8,128)(2,1)}), bf16[32,448,128]{2,1,0:T(8,128)(2,1)}, u32[]{:S(2)}, u32[]{:S(2)}) async-start(bf16[32,448,128]{2,1,0:T(8,128)(2,1)} %shard_map.140), calls=%async_computation | async-start | bytes 7340032 | tf_op jit(solution)/shard_map/all_to_all | solution.py:46
  23.4 0.0 copy-done.8
  23.4 0.0 copy-start.7
  23.4 0.0 copy-done.4
  23.4 0.1 copy.25
  23.5 0.0 copy-done.6
  23.5 0.1 broadcast_multiply_fusion
  23.6 0.2 reduce_window_sum.11
  23.8 0.1 stack.12
  23.9 0.1 stack.14
  24.0 0.1 stack.13
  24.1 0.0 copy-done.3
  24.1 0.3 slice_reduce_fusion.3
  24.4 0.1 fusion.36
  24.5 0.0 copy-done.1
  24.5 2.1 convert_element_type.27
  26.6 0.0 copy-done.7
  26.6 0.1 broadcast_in_dim.31
  26.6 0.1 mul.118
  26.7 0.1 copy.32
  26.8 0.1 copy.33
  26.9 0.1 copy.26
  27.0 0.1 copy.35
  27.1 2.1 broadcast_in_dim.32
  29.2 5.3 %copy.36 = f32[128,7168]{1,0:T(8,128)} copy(f32[128,7168]{0,1:T(8,128)} %bitcast.34) | data formatting | bytes 7340032 | tf_op jit(solution)/shard_map/reshape | solution.py:57
  34.5 2.0 broadcast_in_dim.28
  36.6 5.3 %copy.27 = f32[128,7168]{1,0:T(8,128)} copy(f32[128,7168]{0,1:T(8,128)} %bitcast.35) | data formatting | bytes 7340032 | tf_op jit(solution)/shard_map/reshape | solution.py:57
  41.8 0.0 collective-permute-done
  41.9 0.0 copy-done.5
  41.9 7.4 %multiply_convert_fusion = bf16[128,7424]{1,0:T(8,128)(2,1)S(1)} fusion(f32[128,7424]{1,0:T(8,128)} %convert_element_type.27, f32[3,7424]{1,0:T(4,128)S(1)} %convert_element_type.26, f32[7424]{0:T(1024)S(1)} %get-tuple-element.16, f32[7424]{0:T(1024)S(1)} %get-tuple-element.17, f32[7424]{0:T(1024)S(1)} %get-tuple-element.15, f32[7424]{0:T(1024)S(1)} %get-tuple-element.14, ...), kind=kLoop, calls=%fused_computation.26 | loop fusion | flops 15204352 | bytes 5939200 | tf_op jit(solution)/shard_map/convert_element_type | solution.py:53
  49.3 1.4 slice.72
  50.7 0.1 copy.24
  50.9 0.1 copy.31
  51.0 3.9 %copy.30 = bf16[128,7168]{0,1:T(8,128)(2,1)} copy(bf16[128,7168]{1,0:T(8,128)(2,1)} %slice.72) | data formatting | bytes 3670016 | tf_op jit(solution)/shard_map/slice | solution.py:335
  54.9 0.2 fusion.38
  55.1 10.6 %fusion = f32[2,56,64,128]{3,2,1,0:T(8,128)} fusion(bf16[128,2,56,64]{0,3,2,1:T(8,128)(2,1)} %bitcast.41, f32[2,56,128]{2,1,0:T(8,128)S(1)} %bitcast.49, f32[2,56,128]{2,1,0:T(8,128)S(1)} %bitcast.48, f32[2,128,128]{2,1,0:T(8,128)S(1)} %fusion.38, pred[128,128]{1,0:T(8,128)(4,1)S(1)} %iota_compare_fusion), kind=kOutput, calls=%fused_computation | convolution fusion | flops 1416626176 | bytes 5767168 | tf_op jit(solution)/shard_map/gkts,sgkp->tgkp/dot_general | solution.py:366
  65.7 0.0 copy-done.2
  65.7 5.2 %copy.34 = f32[128,7168]{1,0:T(8,128)} copy(f32[128,7168]{0,1:T(8,128)} %bitcast.39) | data formatting | bytes 7340032 | tf_op jit(solution)/shard_map/reshape | solution.py:368
  70.9 7.6 %fusion.16 = (f32[128,7168]{1,0:T(8,128)}, f32[128,7168]{1,0:T(8,128)S(1)}, f32[128,7168]{1,0:T(8,128)}) fusion(f32[128,7168]{1,0:T(8,128)} %copy.34, f32[7168]{0:T(1024)S(1)} %mul.118, bf16[128,7168]{1,0:T(8,128)(2,1)} %param.14, bf16[128,7424]{1,0:T(8,128)(2,1)S(1)} %multiply_convert_fusion, f32[128,7168]{1,0:T(8,128)} %copy.27, f32[128,7168]{1,0:T(8,128)} %copy.36), kind=kLoop, calls=%fused_computation.28 | loop fusion | flops 10092544 | bytes 25718784 | tf_op jit(solution)/shard_map/mul | solution.py:368
  78.5 0.8 convolution_convert_fusion
  79.3 0.8 convolution_convert_fusion.1
  80.1 0.1 pad_maximum_fusion.2
  80.2 1.2 convert_element_type.30
  81.4 1.1 copy.28
  82.5 0.1 pad_maximum_fusion.1
  82.7 23.8 %all-to-all-done.query_ref.key_ref = bf16[32,448,128]{2,1,0:T(8,128)(2,1)} async-done(((bf16[32,448,128]{2,1,0:T(8,128)(2,1)}), bf16[32,448,128]{2,1,0:T(8,128)(2,1)}, u32[]{:S(2)}, u32[]{:S(2)}) %all-to-all-start) | async-done | bytes 3670048 | tf_op jit(solution)/shard_map/all_to_all | solution.py:46
  106.4 34.0 %all_to_all.25.recv_ref = bf16[32,128,128]{2,1,0:T(8,128)(2,1)} all-to-all(bf16[32,128,128]{2,1,0:T(8,128)(2,1)S(1)} %pad_maximum_fusion.1), channel_id=1, replica_groups=mesh['dp'=8,'ctx'=32] {'ctx'}, dimensions={0} | all-to-all | bytes 2097152 | tf_op jit(solution)/shard_map/all_to_all | solution.py:46
  140.4 2.7 shard_map.141
  143.1 29.7 %all_to_all.26 = bf16[32,112,128]{2,1,0:T(8,128)(2,1)} all-to-all(bf16[32,112,128]{2,1,0:T(8,128)(2,1)} %shard_map.141), channel_id=1, replica_groups=mesh['dp'=8,'ctx'=32] {'ctx'}, dimensions={0} | all-to-all | bytes 1835008 | tf_op jit(solution)/shard_map/all_to_all | solution.py:46
  172.7 9.4 %shard_map.142 = (bf16[128,7168]{1,0:T(8,128)(2,1)}, bf16[32,224,128]{2,1,0:T(8,128)(2,1)}) custom-call(bf16[128,128]{1,0:T(8,128)(2,1)} %copy-done.2, bf16[4,8,112,128]{3,2,1,0:T(8,128)(2,1)} %bitcast.38, f32[128,7168]{1,0:T(8,128)} %get-tuple-element.21.base_ref, f32[128,7168]{1,0:T(8,128)} %get-tuple-element.25.factor_ref, f32[1,7168]{1,0:T(1,128)} %bitcast.50), custom_call_target="tpu_custom_call" | custom-call | tf_op jit(solution)/shard_map/pallas_call | solution.py:164
  182.2 5.4 %all-to-all-start.3 = ((bf16[32,224,128]{2,1,0:T(8,128)(2,1)}), bf16[32,224,128]{2,1,0:T(8,128)(2,1)S(1)}, u32[]{:S(2)}, u32[]{:S(2)}) async-start(bf16[32,224,128]{2,1,0:T(8,128)(2,1)} %get-tuple-element.8), calls=%async_computation.3 | async-start | bytes 3670016 | tf_op jit(solution)/shard_map/all_to_all | solution.py:46
  187.6 23.1 %shard_map.143.weight_ref = bf16[8,4096,512]{2,1,0:T(8,128)(2,1)} custom-call(bf16[32,448,128]{2,1,0:T(8,128)(2,1)} %all-to-all-done.query_ref.key_ref, bf16[32,448,128]{2,1,0:T(8,128)(2,1)} %all-to-all-done.query_ref.key_ref), custom_call_target="tpu_custom_call" | custom-call | tf_op jit(solution)/shard_map/pallas_call | solution.py:246
  210.7 19.9 %all-to-all-done.3.value_ref = bf16[32,224,128]{2,1,0:T(8,128)(2,1)S(1)} async-done(((bf16[32,224,128]{2,1,0:T(8,128)(2,1)}), bf16[32,224,128]{2,1,0:T(8,128)(2,1)S(1)}, u32[]{:S(2)}, u32[]{:S(2)}) %all-to-all-start.3) | async-done | bytes 1835040 | tf_op jit(solution)/shard_map/all_to_all | solution.py:46
  230.6 1.2 copy-done
  231.8 20.8 %shard_map.144 = bf16[32,224,128]{2,1,0:T(8,128)(2,1)} custom-call(s32[20]{0:T(128)} %constant.22.clone.block_ref, s32[20]{0:T(128)} %constant.23.clone.chunk_ref, bf16[32,224,128]{2,1,0:T(8,128)(2,1)} %copy-done, bf16[8,4096,512]{2,1,0:T(8,128)(2,1)} %shard_map.143.weight_ref), custom_call_target="tpu_custom_call" | custom-call | tf_op jit(solution)/shard_map/pallas_call | solution.py:293
  252.7 48.9 %all_to_all.27 = bf16[32,224,128]{2,1,0:T(8,128)(2,1)S(1)} all-to-all(bf16[32,224,128]{2,1,0:T(8,128)(2,1)} %shard_map.144), channel_id=1, replica_groups=mesh['dp'=8,'ctx'=32] {'ctx'}, dimensions={0} | all-to-all | bytes 3670016 | tf_op jit(solution)/shard_map/all_to_all | solution.py:46
  301.6 2.9 copy.37
  (14 shorter events, 0.1 us)
Async XLA Ops:
  1.6 40.3 %collective-permute-start = (bf16[3,7424]{1,0:T(4,128)(2,1)S(1)}, bf16[3,7424]{1,0:T(4,128)(2,1)S(1)}, u32[]{:S(2)}, u32[]{:S(2)}) collective-permute-start(bf16[3,7424]{1,0:T(4,128)(2,1)S(1)} %slice.50), channel_id=1, source_target_pairs={{0,1},{1,2},{2,3},{3,4},{4,5},{5,6},{6,7},{7,8},{8,9},{9,10},{10,1... | collective-permute-start | bytes 133640 | tf_op jit(solution)/shard_map/ppermute | solution.py:42
  12.1 11.3 %copy-start.8 = (f32[112]{0:T(128)S(1)}, f32[112]{0:T(128)}, u32[]{:S(2)}) copy-start(f32[112]{0:T(128)} %param.17) | copy-start | bytes 1348
  12.1 11.4 %copy-start.4 = (f32[128,112]{0,1:T(8,128)S(1)}, f32[128,112]{0,1:T(8,128)}, u32[]{:S(2)}) copy-start(f32[128,112]{0,1:T(8,128)} %param.15) | copy-start | bytes 172036
  12.1 11.5 %copy-start.6 = (f32[112]{0:T(128)S(1)}, f32[112]{0:T(128)}, u32[]{:S(2)}) copy-start(f32[112]{0:T(128)} %param.16) | copy-start | bytes 1348
  12.1 12.0 %copy-start.3 = (f32[4,7424]{1,0:T(4,128)S(1)}, f32[4,7424]{1,0:T(4,128)}, u32[]{:S(2)}) copy-start(f32[4,7424]{1,0:T(4,128)} %param.19) | copy-start | bytes 356356
  12.1 12.4 %copy-start.1 = (bf16[128,7424]{1,0:T(8,128)(2,1)S(1)}, bf16[128,7424]{1,0:T(8,128)(2,1)}, u32[]{:S(2)}) copy-start(bf16[128,7424]{1,0:T(8,128)(2,1)} %param.13) | copy-start | bytes 5701636
  12.1 94.3 %all-to-all-start = ((bf16[32,448,128]{2,1,0:T(8,128)(2,1)}), bf16[32,448,128]{2,1,0:T(8,128)(2,1)}, u32[]{:S(2)}, u32[]{:S(2)}) async-start(bf16[32,448,128]{2,1,0:T(8,128)(2,1)} %shard_map.140), calls=%async_computation | async-start | bytes 7340032 | tf_op jit(solution)/shard_map/all_to_all | solution.py:46
  23.4 3.2 %copy-start.7 = (f32[112]{0:T(128)S(1)}, f32[112]{0:T(128)}, u32[]{:S(2)}) copy-start(f32[112]{0:T(128)} %param.18) | copy-start | bytes 1348
  36.6 5.3 %copy-start.5 = (f32[7424]{0:T(1024)S(1)}, f32[7424]{0:T(1024)}, u32[]{:S(2)}) copy-start(f32[7424]{0:T(1024)} %param.20) | copy-start | bytes 89092
  50.7 14.9 %copy-start.2 = (bf16[128,128]{1,0:T(8,128)(2,1)}, bf16[128,128]{1,0:T(8,128)(2,1)S(1)}, u32[]{:S(2)}) copy-start(bf16[128,128]{1,0:T(8,128)(2,1)S(1)} %get-tuple-element.24.readout_ref) | copy-start | bytes 98308
  182.2 48.5 %all-to-all-start.3 = ((bf16[32,224,128]{2,1,0:T(8,128)(2,1)}), bf16[32,224,128]{2,1,0:T(8,128)(2,1)S(1)}, u32[]{:S(2)}, u32[]{:S(2)}) async-start(bf16[32,224,128]{2,1,0:T(8,128)(2,1)} %get-tuple-element.8), calls=%async_computation.3 | async-start | bytes 3670016 | tf_op jit(solution)/shard_map/all_to_all | solution.py:46
  230.6 1.2 copy-start
